TPU v7x, 512 devices: a whole 4x4x16 slice. The times are simulated.
512 devices in a mesh: inst: 64 (over x, z), tp: 8 (over y, core).
Axes of the slice: x: 4, y: 4, z: 16, core: 2. Of those that a mesh axis runs over, the one named last changes fastest.
Arguments:
- queries: bfloat16 [256, 2, 4096], P('inst', None, 'tp'), may hold values from -120 to 120
- keys_new: bfloat16 [256, 2, 1024], P('inst', None, 'tp'), may hold values from -6 to 6
- values_new: bfloat16 [256, 2, 1024], P('inst', None, 'tp'), may hold values from -6 to 6
- key_cache: bfloat16 [192, 1024, 1024], P('inst', None, 'tp'), may hold values from -6 to 6
- value_cache: bfloat16 [192, 1024, 1024], P('inst', None, 'tp'), may hold values from -6 to 6
- lengths: int32 [192], replicated, may hold values from 128 to 1022, as said below
- migration: int32 [64, 2], replicated, may hold values from 0 to 63, as said below
- out_weight: bfloat16 [4096, 3072], P('tp'), may hold values from -1.5 to 1.5
Outputs:
- attended: bfloat16 [256, 2, 3072], P('inst', None, 'tp')
- key_out: bfloat16 [256, 1024, 1024], P('inst', None, 'tp')
- value_out: bfloat16 [256, 1024, 1024], P('inst', None, 'tp')
Inputs may be any that keep to these rules, and one draw needn't show every extreme that they name: `lengths`: at least one request has length 1022. `migration`: column 0 is a resident slot below 3; column 1 holds every instance once.
All inputs are finite; a program needn't handle non-finite values.
Results may differ from a plain program's by a relative error of at most 0.012.
The roundings to bfloat16 on the way count: a program that leaves them out, or rounds other values in their place, can miss the bound.
Values may be sent and summed in bfloat16 or wider, within the bound.
A program may use at most 64 MiB of HBM per device.

v0:
```python
import jax
import jax.numpy as jnp
from jax import lax
from jax.sharding import PartitionSpec as P

HEAD_DIM = 128


theta_base = 1000000.0


def rotate(values_in, positions):
    half_size = values_in.shape[-1] // 2
    frequency = jnp.exp(
        -jnp.log(theta_base) * 2.0 * jnp.arange(half_size, dtype=jnp.float32) / values_in.shape[-1]
    )
    angles = positions[:, :, None, None] * frequency[None, None, None, :]
    cosine_part = jnp.concatenate([jnp.cos(angles), jnp.cos(angles)], axis=-1)
    sine_part = jnp.concatenate([jnp.sin(angles), jnp.sin(angles)], axis=-1)
    rotated = jnp.concatenate([-values_in[..., half_size:], values_in[..., :half_size]], axis=-1)
    return values_in * cosine_part + rotated * sine_part


def rotate_keys(key_new, length):
    batch_rows, step_count, kv_width = key_new.shape
    groups = kv_width // HEAD_DIM
    positions = (length[:, None] + jnp.arange(step_count, dtype=jnp.int32)[None, :]).astype(
        jnp.float32
    )
    return (
        rotate(
            key_new.astype(jnp.float32).reshape(batch_rows, step_count, groups, HEAD_DIM), positions
        )
        .astype(jnp.bfloat16)
        .reshape(batch_rows, step_count, kv_width)
    )


def attend(query, key_new, value_new, key_cache, value_cache, length):
    batch_rows, step_count, query_width = query.shape
    kv_width = key_new.shape[-1]
    groups = kv_width // HEAD_DIM
    group_size = query_width // kv_width
    window = key_cache.shape[1]
    positions = (length[:, None] + jnp.arange(step_count, dtype=jnp.int32)[None, :]).astype(
        jnp.float32
    )
    query_rot = rotate(
        query.astype(jnp.float32).reshape(batch_rows, step_count, groups * group_size, HEAD_DIM),
        positions,
    ).astype(jnp.bfloat16)
    key_flat = rotate_keys(key_new, length)
    key_rot = key_flat.reshape(batch_rows, step_count, groups, HEAD_DIM)
    query_rot = query_rot.reshape(batch_rows, step_count, groups, group_size, HEAD_DIM)
    cache_keys = key_cache.reshape(batch_rows, window, groups, HEAD_DIM)
    cache_values = value_cache.reshape(batch_rows, window, groups, HEAD_DIM)
    fresh_values = value_new.reshape(batch_rows, step_count, groups, HEAD_DIM)
    score_scale = HEAD_DIM ** (-0.5)
    cache_scores = (
        jnp.einsum("stgrd,slgd->stgrl", query_rot, cache_keys, preferred_element_type=jnp.float32)
        * score_scale
    )
    new_scores = (
        jnp.einsum("stgrd,sugd->stgru", query_rot, key_rot, preferred_element_type=jnp.float32)
        * score_scale
    )
    live_cache = jnp.arange(window, dtype=jnp.int32)[None, :] < length[:, None]
    live_new = jnp.arange(step_count)[None, :] <= jnp.arange(step_count)[:, None]
    cache_scores = jnp.where(live_cache[:, None, None, None, :], cache_scores, -1e30)
    new_scores = jnp.where(live_new[None, :, None, None, :], new_scores, -1e30)
    row_top = jnp.maximum(jnp.max(cache_scores, axis=-1), jnp.max(new_scores, axis=-1))[..., None]
    cache_exp = jnp.exp(cache_scores - row_top)
    new_exp = jnp.exp(new_scores - row_top)
    denominator = jnp.sum(cache_exp, axis=-1, keepdims=True) + jnp.sum(
        new_exp, axis=-1, keepdims=True
    )
    cache_probs = (cache_exp / denominator).astype(jnp.bfloat16)
    new_probs = (new_exp / denominator).astype(jnp.bfloat16)
    mixed = jnp.einsum(
        "stgrl,slgd->stgrd", cache_probs, cache_values, preferred_element_type=jnp.float32
    )
    mixed = mixed + jnp.einsum(
        "stgru,sugd->stgrd", new_probs, fresh_values, preferred_element_type=jnp.float32
    )
    return (mixed.reshape(batch_rows, step_count, query_width).astype(jnp.bfloat16), key_flat)


def write_steps(cache, fresh, length):
    zero_index = jnp.zeros((), jnp.int32)

    def write_one(cache_row, fresh_row, start):
        return lax.dynamic_update_slice(cache_row, fresh_row, (start, zero_index))

    return jax.vmap(write_one)(cache, fresh, length)


def local(queries, keys_new, values_new, key_cache, value_cache, lengths, migration, out_weight):
    inst_count = lax.axis_size("inst")
    own_index = lax.axis_index("inst")
    resident = key_cache.shape[0]
    window = key_cache.shape[1]
    kv_width = key_cache.shape[2]
    instances = jnp.arange(inst_count, dtype=jnp.int32)
    slots_out = migration[:, 0]
    targets = migration[:, 1]
    anchor = jnp.sum(
        jnp.where(targets[:, None] == instances[None, :], instances[:, None], 0), axis=0
    )
    leaving = lax.dynamic_index_in_dim(slots_out, own_index, 0, keepdims=False)
    own_lengths = lax.dynamic_slice_in_dim(lengths, own_index * resident, resident)
    kept_lengths = jnp.where(jnp.arange(resident, dtype=jnp.int32) == leaving, 0, own_lengths)
    source = lax.dynamic_index_in_dim(anchor, own_index, 0, keepdims=False)
    source_slot = lax.dynamic_index_in_dim(slots_out, source, 0, keepdims=False)
    arriving_length = lax.dynamic_index_in_dim(
        lengths, source * resident + source_slot, 0, keepdims=True
    )
    staying, staying_keys = attend(
        queries[:resident],
        keys_new[:resident],
        values_new[:resident],
        key_cache,
        value_cache,
        kept_lengths,
    )
    piece_rows = window // inst_count
    moving_keys = lax.dynamic_index_in_dim(key_cache, leaving, 0, keepdims=False).reshape(
        inst_count, piece_rows, kv_width
    )
    moving_values = lax.dynamic_index_in_dim(value_cache, leaving, 0, keepdims=False).reshape(
        inst_count, piece_rows, kv_width
    )
    spread_keys, spread_values = (
        lax.all_to_all(moving_keys, "inst", split_axis=0, concat_axis=0, tiled=True),
        lax.all_to_all(moving_values, "inst", split_axis=0, concat_axis=0, tiled=True),
    )
    ordered_keys = jnp.take(spread_keys, anchor, axis=0)
    ordered_values = jnp.take(spread_values, anchor, axis=0)
    arrived_keys, arrived_values = (
        lax.all_to_all(ordered_keys, "inst", split_axis=0, concat_axis=0, tiled=True),
        lax.all_to_all(ordered_values, "inst", split_axis=0, concat_axis=0, tiled=True),
    )
    arrived_keys = arrived_keys.reshape(1, window, kv_width)
    arrived_values = arrived_values.reshape(1, window, kv_width)
    landing, landing_keys = attend(
        queries[resident:],
        keys_new[resident:],
        values_new[resident:],
        arrived_keys,
        arrived_values,
        arriving_length,
    )
    all_lengths = jnp.concatenate([kept_lengths, arriving_length], axis=0)
    key_rows = jnp.concatenate([key_cache, arrived_keys], axis=0)
    value_rows = jnp.concatenate([value_cache, arrived_values], axis=0)
    key_out = write_steps(
        key_rows, jnp.concatenate([staying_keys, landing_keys], axis=0), all_lengths
    )
    value_out = write_steps(value_rows, values_new, all_lengths)
    mixed = jnp.concatenate([staying, landing], axis=0)
    partial_value = jnp.einsum("stq,qd->std", mixed, out_weight, preferred_element_type=jnp.float32)
    summed = lax.psum(partial_value, "tp")
    share_cols = summed.shape[2] // lax.axis_size("tp")
    result = lax.dynamic_slice_in_dim(summed, lax.axis_index("tp") * share_cols, share_cols, 2)
    return (result.astype(jnp.bfloat16), key_out, value_out)


def solution(mesh):
    in_specs = (
        P("inst", None, "tp"),
        P("inst", None, "tp"),
        P("inst", None, "tp"),
        P("inst", None, "tp"),
        P("inst", None, "tp"),
        P(),
        P(),
        P("tp", None),
    )
    out_specs = (P("inst", None, "tp"), P("inst", None, "tp"), P("inst", None, "tp"))
    return jax.shard_map(local, mesh=mesh, in_specs=in_specs, out_specs=out_specs, check_vma=False)
```

profile of v0, /device:TPU:1, one launch (start us, length us, event | category | flops | bytes accessed | tf_op | source)
XLA Modules:
  0.0 247.6 jit_solution(5000545434002009320)
XLA Ops:
  8.3 19.1 %all-to-all-start.2 = ((bf16[64,16,128]{2,1,0:T(8,128)(2,1)}), bf16[64,16,128]{2,1,0:T(8,128)(2,1)S(1)}, u32[]{:S(2)}, u32[]{:S(2)}) async-start(bf16[64,16,128]{2,1,0:T(8,128)(2,1)} %bitcast.188), calls=%async_computation.2 | async-start | bytes 524288 | tf_op jit(solution)/shard_map/all_to_all | solution.py:133
  46.6 14.8 %all-to-all-start = ((bf16[64,16,128]{2,1,0:T(8,128)(2,1)}), bf16[64,16,128]{2,1,0:T(8,128)(2,1)}, u32[]{:S(2)}, u32[]{:S(2)}) async-start(bf16[64,16,128]{2,1,0:T(8,128)(2,1)} %bitcast.189), calls=%async_computation | async-start | bytes 524288 | tf_op jit(solution)/shard_map/all_to_all | solution.py:134
  68.4 11.3 %all-to-all-done = bf16[64,16,128]{2,1,0:T(8,128)(2,1)} async-done(((bf16[64,16,128]{2,1,0:T(8,128)(2,1)}), bf16[64,16,128]{2,1,0:T(8,128)(2,1)}, u32[]{:S(2)}, u32[]{:S(2)}) %all-to-all-start) | async-done | bytes 262176 | tf_op jit(solution)/shard_map/all_to_all | solution.py:134
  83.2 7.8 %all-to-all-start.3 = ((bf16[64,16,128]{2,1,0:T(8,128)(2,1)}), bf16[64,16,128]{2,1,0:T(8,128)(2,1)S(1)}, u32[]{:S(2)}, u32[]{:S(2)}) async-start(bf16[64,16,128]{2,1,0:T(8,128)(2,1)} %get-tuple-element.82), calls=%async_computation.3 | async-start | bytes 524288 | tf_op jit(solution)/shard_map/all_to_all | solution.py:139
  94.7 14.1 %all-to-all-done.3 = bf16[64,16,128]{2,1,0:T(8,128)(2,1)S(1)} async-done(((bf16[64,16,128]{2,1,0:T(8,128)(2,1)}), bf16[64,16,128]{2,1,0:T(8,128)(2,1)S(1)}, u32[]{:S(2)}, u32[]{:S(2)}) %all-to-all-start.3) | async-done | bytes 262176 | tf_op jit(solution)/shard_map/all_to_all | solution.py:139
  108.8 8.2 %all-to-all-start.1 = ((bf16[64,16,128]{2,1,0:T(8,128)(2,1)}), bf16[64,16,128]{2,1,0:T(8,128)(2,1)}, u32[]{:S(2)}, u32[]{:S(2)}) async-start(bf16[64,16,128]{2,1,0:T(8,128)(2,1)} %get-tuple-element.83), calls=%async_computation.1 | async-start | bytes 524288 | tf_op jit(solution)/shard_map/all_to_all | solution.py:140
  119.1 14.9 %all-to-all-done.1 = bf16[64,16,128]{2,1,0:T(8,128)(2,1)} async-done(((bf16[64,16,128]{2,1,0:T(8,128)(2,1)}), bf16[64,16,128]{2,1,0:T(8,128)(2,1)}, u32[]{:S(2)}, u32[]{:S(2)}) %all-to-all-start.1) | async-done | bytes 262176 | tf_op jit(solution)/shard_map/all_to_all | solution.py:140
  136.6 26.0 %psum.7 = bf16[4,2,3072]{2,0,1:T(4,128)(2,1)S(1)} all-reduce(f32[4,2,3072]{2,0,1:T(4,128)S(1)} %fusion), channel_id=1, replica_groups=mesh['inst'=64,'tp'=8] {'tp'}, use_global_device_ids=true, to_apply=%region_9.11 | all-reduce | flops 24576 | bytes 147456 | tf_op jit(solution)/shard_map/psum | solution.py:161
  165.5 40.2 %while.2 = (s32[]{:T(128)}, bf16[4,1024,128]{2,1,0:T(8,128)(2,1)}, s32[4,3]{1,0:T(4,128)}, bf16[4,2,128]{2,1,0:T(2,128)(2,1)}, s32[]{:T(128)}, /*index=5*/s32[3]{0:T(128)}, s32[]{:T(128)}) while((s32[]{:T(128)}, bf16[4,1024,128]{2,1,0:T(8,128)(2,1)}, s32[4,3]{1,0:T(4,128)}, bf16[4,2,128]{2,1,0:T(2,128)(2,1)}, s32[]{:T(128)}, /*index=5*/s32[3]{0:T(128)}, ...), condition=%wide.while_cond, body=%wide.while_body.sunk | while | flops 275 | bytes 2739 | solution.py:92
  166.8 3.3 %and_reduce_fusion.4 = pred[]{:T(512)} fusion(s32[3]{0:T(128)} %get-tuple-element.173, s32[1]{0:T(128)} %bitcast.176, s32[1]{0:T(128)} %bitcast.177, s32[1]{0:T(128)} %bitcast.178), kind=kLoop, calls=%fused_computation.2.clone.1 | loop fusion | flops 17 | bytes 25 | tf_op jit(solution)/shard_map/vmap(vmap())/scatter
  170.1 2.7 %broadcast_select_fusion.6 = bf16[1,2,128]{2,1,0:T(2,128)(2,1)S(1)} fusion(pred[]{:T(512)} %and_reduce_fusion.4, bf16[4,2,128]{2,1,0:T(2,128)(2,1)} %get-tuple-element.171, s32[]{:T(128)S(6)} %copy.59, bf16[4,1024,128]{2,1,0:T(8,128)(2,1)} %get-tuple-element.162, s32[]{:T(128)} %bitcast.179, s32[]{:T(128)} %bitcast.180), kind=kLoop, calls=%fused_computation.3.clone.1 | loop fusion | flops 256 | bytes 1549 | tf_op jit(solution)/shard_map/vmap(vmap())/scatter
  176.8 3.3 %and_reduce_fusion.4 = pred[]{:T(512)} fusion(s32[3]{0:T(128)} %get-tuple-element.173, s32[1]{0:T(128)} %bitcast.176, s32[1]{0:T(128)} %bitcast.177, s32[1]{0:T(128)} %bitcast.178), kind=kLoop, calls=%fused_computation.2.clone.1 | loop fusion | flops 17 | bytes 25 | tf_op jit(solution)/shard_map/vmap(vmap())/scatter
  180.1 2.7 %broadcast_select_fusion.6 = bf16[1,2,128]{2,1,0:T(2,128)(2,1)S(1)} fusion(pred[]{:T(512)} %and_reduce_fusion.4, bf16[4,2,128]{2,1,0:T(2,128)(2,1)} %get-tuple-element.171, s32[]{:T(128)S(6)} %copy.59, bf16[4,1024,128]{2,1,0:T(8,128)(2,1)} %get-tuple-element.162, s32[]{:T(128)} %bitcast.179, s32[]{:T(128)} %bitcast.180), kind=kLoop, calls=%fused_computation.3.clone.1 | loop fusion | flops 256 | bytes 1549 | tf_op jit(solution)/shard_map/vmap(vmap())/scatter
  186.9 3.3 %and_reduce_fusion.4 = pred[]{:T(512)} fusion(s32[3]{0:T(128)} %get-tuple-element.173, s32[1]{0:T(128)} %bitcast.176, s32[1]{0:T(128)} %bitcast.177, s32[1]{0:T(128)} %bitcast.178), kind=kLoop, calls=%fused_computation.2.clone.1 | loop fusion | flops 17 | bytes 25 | tf_op jit(solution)/shard_map/vmap(vmap())/scatter
  190.2 2.7 %broadcast_select_fusion.6 = bf16[1,2,128]{2,1,0:T(2,128)(2,1)S(1)} fusion(pred[]{:T(512)} %and_reduce_fusion.4, bf16[4,2,128]{2,1,0:T(2,128)(2,1)} %get-tuple-element.171, s32[]{:T(128)S(6)} %copy.59, bf16[4,1024,128]{2,1,0:T(8,128)(2,1)} %get-tuple-element.162, s32[]{:T(128)} %bitcast.179, s32[]{:T(128)} %bitcast.180), kind=kLoop, calls=%fused_computation.3.clone.1 | loop fusion | flops 256 | bytes 1549 | tf_op jit(solution)/shard_map/vmap(vmap())/scatter
  192.9 2.7 %dynamic-update-slice.6 = bf16[4,1024,128]{2,1,0:T(8,128)(2,1)} dynamic-update-slice(bf16[4,1024,128]{2,1,0:T(8,128)(2,1)} %get-tuple-element.162, bf16[1,2,128]{2,1,0:T(2,128)(2,1)S(1)} %broadcast_select_fusion.6, s32[]{:T(128)} %bitcast.179, s32[]{:T(128)} %bitcast.180, s32[]{:T(128)} %constant.30.clone.1..sunk) | dynamic-update-slice | bytes 1028 | tf_op jit(solution)/shard_map/vmap(vmap())/scatter
  196.9 3.3 %and_reduce_fusion.4 = pred[]{:T(512)} fusion(s32[3]{0:T(128)} %get-tuple-element.173, s32[1]{0:T(128)} %bitcast.176, s32[1]{0:T(128)} %bitcast.177, s32[1]{0:T(128)} %bitcast.178), kind=kLoop, calls=%fused_computation.2.clone.1 | loop fusion | flops 17 | bytes 25 | tf_op jit(solution)/shard_map/vmap(vmap())/scatter
  200.2 2.7 %broadcast_select_fusion.6 = bf16[1,2,128]{2,1,0:T(2,128)(2,1)S(1)} fusion(pred[]{:T(512)} %and_reduce_fusion.4, bf16[4,2,128]{2,1,0:T(2,128)(2,1)} %get-tuple-element.171, s32[]{:T(128)S(6)} %copy.59, bf16[4,1024,128]{2,1,0:T(8,128)(2,1)} %get-tuple-element.162, s32[]{:T(128)} %bitcast.179, s32[]{:T(128)} %bitcast.180), kind=kLoop, calls=%fused_computation.3.clone.1 | loop fusion | flops 256 | bytes 1549 | tf_op jit(solution)/shard_map/vmap(vmap())/scatter
  202.9 2.7 %dynamic-update-slice.6 = bf16[4,1024,128]{2,1,0:T(8,128)(2,1)} dynamic-update-slice(bf16[4,1024,128]{2,1,0:T(8,128)(2,1)} %get-tuple-element.162, bf16[1,2,128]{2,1,0:T(2,128)(2,1)S(1)} %broadcast_select_fusion.6, s32[]{:T(128)} %bitcast.179, s32[]{:T(128)} %bitcast.180, s32[]{:T(128)} %constant.30.clone.1..sunk) | dynamic-update-slice | bytes 1028 | tf_op jit(solution)/shard_map/vmap(vmap())/scatter
  207.9 39.7 %while.3 = (s32[]{:T(128)}, bf16[4,1024,128]{2,1,0:T(8,128)(2,1)}, s32[4,3]{1,0:T(4,128)}, bf16[4,2,128]{2,1,0:T(2,128)(2,1)}, s32[]{:T(128)}, /*index=5*/s32[3]{0:T(128)}, s32[]{:T(128)}) while((s32[]{:T(128)}, bf16[4,1024,128]{2,1,0:T(8,128)(2,1)}, s32[4,3]{1,0:T(4,128)}, bf16[4,2,128]{2,1,0:T(2,128)(2,1)}, s32[]{:T(128)}, /*index=5*/s32[3]{0:T(128)}, ...), condition=%wide.while_cond.1, body=%wide.while_body.1.sunk | while | flops 275 | bytes 2739 | solution.py:92
  209.2 3.3 %and_reduce_fusion.5 = pred[]{:T(512)} fusion(s32[3]{0:T(128)} %get-tuple-element.194, s32[1]{0:T(128)} %bitcast.181, s32[1]{0:T(128)} %bitcast.182, s32[1]{0:T(128)} %bitcast.183), kind=kLoop, calls=%fused_computation.7.clone.1 | loop fusion | flops 17 | bytes 25 | tf_op jit(solution)/shard_map/vmap(vmap())/scatter
  219.2 3.3 %and_reduce_fusion.5 = pred[]{:T(512)} fusion(s32[3]{0:T(128)} %get-tuple-element.194, s32[1]{0:T(128)} %bitcast.181, s32[1]{0:T(128)} %bitcast.182, s32[1]{0:T(128)} %bitcast.183), kind=kLoop, calls=%fused_computation.7.clone.1 | loop fusion | flops 17 | bytes 25 | tf_op jit(solution)/shard_map/vmap(vmap())/scatter
  229.1 3.3 %and_reduce_fusion.5 = pred[]{:T(512)} fusion(s32[3]{0:T(128)} %get-tuple-element.194, s32[1]{0:T(128)} %bitcast.181, s32[1]{0:T(128)} %bitcast.182, s32[1]{0:T(128)} %bitcast.183), kind=kLoop, calls=%fused_computation.7.clone.1 | loop fusion | flops 17 | bytes 25 | tf_op jit(solution)/shard_map/vmap(vmap())/scatter
  239.0 3.3 %and_reduce_fusion.5 = pred[]{:T(512)} fusion(s32[3]{0:T(128)} %get-tuple-element.194, s32[1]{0:T(128)} %bitcast.181, s32[1]{0:T(128)} %bitcast.182, s32[1]{0:T(128)} %bitcast.183), kind=kLoop, calls=%fused_computation.7.clone.1 | loop fusion | flops 17 | bytes 25 | tf_op jit(solution)/shard_map/vmap(vmap())/scatter
  (110 shorter events, 82.7 us)
Async XLA Ops:
  0.6 135.5 %copy-start = (bf16[512,3072]{1,0:T(8,128)(2,1)S(1)}, bf16[512,3072]{1,0:T(8,128)(2,1)}, u32[]{:S(2)}) copy-start(bf16[512,3072]{1,0:T(8,128)(2,1)} %param.17) | copy-start | bytes 9437188
  8.3 38.3 %all-to-all-start.2 = ((bf16[64,16,128]{2,1,0:T(8,128)(2,1)}), bf16[64,16,128]{2,1,0:T(8,128)(2,1)S(1)}, u32[]{:S(2)}, u32[]{:S(2)}) async-start(bf16[64,16,128]{2,1,0:T(8,128)(2,1)} %bitcast.188), calls=%async_computation.2 | async-start | bytes 524288 | tf_op jit(solution)/shard_map/all_to_all | solution.py:133
  46.6 33.1 %all-to-all-start = ((bf16[64,16,128]{2,1,0:T(8,128)(2,1)}), bf16[64,16,128]{2,1,0:T(8,128)(2,1)}, u32[]{:S(2)}, u32[]{:S(2)}) async-start(bf16[64,16,128]{2,1,0:T(8,128)(2,1)} %bitcast.189), calls=%async_computation | async-start | bytes 524288 | tf_op jit(solution)/shard_map/all_to_all | solution.py:134
  83.2 25.6 %all-to-all-start.3 = ((bf16[64,16,128]{2,1,0:T(8,128)(2,1)}), bf16[64,16,128]{2,1,0:T(8,128)(2,1)S(1)}, u32[]{:S(2)}, u32[]{:S(2)}) async-start(bf16[64,16,128]{2,1,0:T(8,128)(2,1)} %get-tuple-element.82), calls=%async_computation.3 | async-start | bytes 524288 | tf_op jit(solution)/shard_map/all_to_all | solution.py:139
  108.8 25.3 %all-to-all-start.1 = ((bf16[64,16,128]{2,1,0:T(8,128)(2,1)}), bf16[64,16,128]{2,1,0:T(8,128)(2,1)}, u32[]{:S(2)}, u32[]{:S(2)}) async-start(bf16[64,16,128]{2,1,0:T(8,128)(2,1)} %get-tuple-element.83), calls=%async_computation.1 | async-start | bytes 524288 | tf_op jit(solution)/shard_map/all_to_all | solution.py:140
where the time goes:
time: 252 us; the launch traced here: 248 us
  other arithmetic  74.7 us (30%)
  starting transfers between devices  50 us (20%)
  local copies, waits for them, and re-layouts  43.6 us (17%)
  waiting for transfers between devices  40.4 us (16%)
  blocking collectives  26 us (10%)
  matrix products  6.97 us (3%)
  between operations  5.96 us (2%)
    scatter x16, other arithmetic  47.9 us
    scatter x24, local copies, waits for them, and re-layouts  32 us
    psum x1, blocking collectives, local(): summed = lax.psum(partial_value, 'tp')  26 us
    all_to_all x1, starting transfers between devices, local(): lax.all_to_all(moving_keys, 'inst', split_axis=0, concat_axis=0, tiled=True)  19.1 us
    all_to_all x1, waiting for transfers between devices, local(): lax.all_to_all(ordered_values, 'inst', split_axis=0, concat_axis=0, tiled...  14.9 us
    all_to_all x1, starting transfers between devices, local(): lax.all_to_all(moving_values, 'inst', split_axis=0, concat_axis=0, tiled=...  14.8 us
    all_to_all x1, waiting for transfers between devices, local(): lax.all_to_all(ordered_keys, 'inst', split_axis=0, concat_axis=0, tiled=T...  14.1 us
    all_to_all x1, waiting for transfers between devices, local(): lax.all_to_all(moving_values, 'inst', split_axis=0, concat_axis=0, tiled=...  11.3 us
  transfers between devices with their start and end apart: 4, of which 3 were waited for; matrix products, arithmetic and copies ran while one was open for 12% of the time, Pallas kernels for 0%

commit v1 on v0

v1 whole, which is shorter than its diff:
```python
import functools

import jax
import jax.numpy as jnp
from jax import lax
from jax.experimental import pallas as pl
from jax.experimental.pallas import tpu as pltpu
from jax.sharding import PartitionSpec as P

MESH = pl.DeviceIdType.MESH
HEAD = 128
THETA = 1000000.0
XS, ZS = 4, 16
INST = XS * ZS
TP = 8
RES = 3
WINDOW = 1024
PIECE = WINDOW // INST
STEPS = 2
HEADS = 4
F32 = jnp.float32
BF16 = jnp.bfloat16


def peer(j, x, z):
    dx = 3 - lax.rem(j, 4)
    t = 15 - j // 4
    dz = lax.rem(jnp.where(lax.rem(t, 2) == 1, (t + 1) // 2, ZS - t // 2), ZS)
    return dx * ZS + dz, lax.rem(x + dx, XS) * ZS + lax.rem(z + dz, ZS)


def rows_of(i):
    return pl.ds(pl.multiple_of(i * PIECE, PIECE), PIECE)


def rotate(v, cos, sin):
    lane = lax.broadcasted_iota(jnp.int32, v.shape, 1)
    turned = pltpu.roll(v, HEAD // 2, 1)
    return v * cos + jnp.where(lane < HEAD // 2, -turned, turned) * sin


def kernel(
    lengths_h, mig_h, queries_h, keys_h, values_h, kc, vc, w,
    attended, ko, vo,
    lengths, mig, mig_v, queries, keys_new, values_new,
    res_k, res_v, arr, stage, spread_k, spread_v, ordered, wv, plan_v, plan,
    qr, kr, prob, fresh, mixed, part, got, part_l, got_l,
    i_sem, a_sem, s_sem, r_sem, o_sem, p_send, p_recv,
):
    res, spread = (res_k, res_v), (spread_k, spread_v)
    me = lax.axis_index("inst")
    tp = lax.axis_index("tp")
    x, z = me // ZS, lax.rem(me, ZS)

    barrier = pltpu.get_barrier_semaphore()

    def greet(j, _):
        _, d = peer(j, x, z)
        pl.semaphore_signal(barrier, inc=1, device_id={"inst": d}, device_id_type=MESH)
        return 0

    lax.fori_loop(0, INST - 1, greet, 0)

    def greet_tp(j, _):
        pl.semaphore_signal(barrier, inc=1, device_id={"tp": lax.rem(tp + j, TP)}, device_id_type=MESH)
        return 0

    lax.fori_loop(1, TP, greet_tp, 0)

    pairs = [
        (mig_h, mig), (kc, res_k), (vc, res_v), (mig_h, mig_v), (lengths_h, lengths),
        (queries_h, queries), (keys_h, keys_new), (values_h, values_new), (w, wv),
    ]
    loads = [pltpu.make_async_copy(src, dst, i_sem.at[i]) for i, (src, dst) in enumerate(pairs)]
    for load in loads:
        load.start()

    def send_first(c):
        def step(j, _):
            o, d = peer(j, x, z)
            pltpu.make_async_remote_copy(
                stage.at[c, rows_of(d)], spread[c].at[o], s_sem.at[0, c], r_sem.at[0, c],
                device_id={"inst": d}, device_id_type=MESH,
            ).start()
            return 0

        lax.fori_loop(0, INST - 1, step, 0)
        spread[c][0] = stage[c, rows_of(me)]

    def send_second(c):
        def pick(d, _):
            ordered[c, rows_of(d)] = spread[c][plan[d, 1]]
            return 0

        lax.fori_loop(0, INST, pick, 0)

        def step(j, _):
            _, d = peer(j, x, z)
            pltpu.make_async_remote_copy(
                ordered.at[c, rows_of(d)], arr.at[c, rows_of(me)], s_sem.at[1, c], r_sem.at[1, c],
                device_id={"inst": d}, device_id_type=MESH,
            ).start()
            return 0

        lax.fori_loop(0, INST - 1, step, 0)
        arr[c, rows_of(me)] = ordered[c, rows_of(me)]

    def wait_bytes(sem, buf):
        pltpu.make_async_copy(buf, buf, sem).wait()

    sent = pl.ds(0, (INST - 1) * PIECE)
    loads[0].wait()
    leaving = mig[0, me]
    for c in range(2):
        loads[1 + c].wait()
        stage[c] = res[c][leaving]
    pl.semaphore_wait(barrier, INST - 1 + TP - 1)
    for c in range(2):
        send_first(c)
    for load in loads[3:8]:
        load.wait()

    s_of = lax.broadcasted_iota(jnp.int32, (INST, INST), 1)
    d_of = lax.broadcasted_iota(jnp.int32, (INST, INST), 0)
    anchor = jnp.max(jnp.where(mig_v[1:2, :] == d_of, s_of, 0), axis=1, keepdims=True)
    slot = ((x - lax.shift_right_logical(anchor, 4)) & (XS - 1)) * ZS + ((z - anchor) & (ZS - 1))
    column = lax.broadcasted_iota(jnp.int32, plan_v.shape, 1)
    plan_v[...] = jnp.where(column == 0, anchor, slot)
    to_smem = pltpu.make_async_copy(plan_v, plan, a_sem)
    to_smem.start()
    to_smem.wait()

    source = plan[me, 0]
    ctx = [jnp.where(leaving == k, 0, lengths[me * RES + k]) for k in range(RES)]
    ctx.append(lengths[source * RES + mig[0, source]])
    n_q = (RES + 1) * HEADS * STEPS
    row = lax.broadcasted_iota(jnp.int32, (n_q, HEAD), 0)
    freq_at = lax.rem(lax.broadcasted_iota(jnp.int32, (n_q, HEAD), 1), HEAD // 2).astype(F32)
    freq = jnp.exp(-jnp.log(jnp.float32(THETA)) * 2.0 * freq_at / HEAD)
    per = HEADS * STEPS
    pos = lax.rem(row, STEPS)
    for r in range(RES + 1):
        pos = pos + jnp.where(row // per == r, ctx[r], 0)
    angle = pos.astype(F32) * freq
    cos, sin = jnp.cos(angle), jnp.sin(angle)
    heads = []
    for r in range(RES + 1):
        flat = queries[r].astype(F32)
        heads += [flat[:, h * HEAD : (h + 1) * HEAD] for h in range(HEADS)]
    qr[...] = rotate(jnp.concatenate(heads, axis=0), cos, sin).astype(BF16).astype(F32)
    k_flat = jnp.concatenate([keys_new[r].astype(F32) for r in range(RES + 1)], axis=0)
    k_cos = jnp.concatenate([cos[r * per : r * per + STEPS] for r in range(RES + 1)], axis=0)
    k_sin = jnp.concatenate([sin[r * per : r * per + STEPS] for r in range(RES + 1)], axis=0)
    kr[...] = rotate(k_flat, k_cos, k_sin).astype(BF16).astype(F32)

    def write_tokens(r, c, buf):
        both = values_new[r].astype(F32) if c else kr[pl.ds(r * STEPS, STEPS), :]
        block = 128

        def step(i, _):
            at = pl.ds(pl.multiple_of(i * block, block), block)
            place = lax.broadcasted_iota(jnp.int32, (block, HEAD), 0) + i * block - ctx[r]
            old = buf[at, :].astype(F32)
            buf[at, :] = jnp.where(place == 0, both[0:1], jnp.where(place == 1, both[1:2], old)).astype(BF16)
            return 0

        lax.fori_loop(0, WINDOW // block, step, 0)
        pltpu.make_async_copy(buf, (ko, vo)[c].at[r], o_sem.at[c, r]).start()

    def weigh(r, keys):
        q = qr[pl.ds(r * per, per), :].astype(BF16)
        s = lax.dot_general(q, keys[...], (((1,), (1,)), ((), ())), preferred_element_type=F32)
        s = s * (HEAD**-0.5)
        place = lax.broadcasted_iota(jnp.int32, s.shape, 1) - ctx[r]
        step = lax.rem(lax.broadcasted_iota(jnp.int32, s.shape, 0), STEPS)
        s = jnp.where(place <= step, s, -1e30)
        e = jnp.exp(s - jnp.max(s, axis=1, keepdims=True))
        p = (e / jnp.sum(e, axis=1, keepdims=True)).astype(BF16).astype(F32)
        prob[r] = jnp.where(place < 0, p, 0.0)
        for t in range(STEPS):
            fresh[t] = jnp.broadcast_to(jnp.sum(jnp.where(place == t, p, 0.0), axis=1, keepdims=True), fresh.shape[1:])

    def mix(r, values, at):
        o = jnp.dot(prob[r].astype(BF16), values[...], preferred_element_type=F32)
        both = values_new[r].astype(F32)
        for t in range(STEPS):
            o = o + fresh[t] * both[t : t + 1]
        for h in range(HEADS):
            mixed[pl.ds(at, STEPS), pl.ds(h * HEAD, HEAD)] = o[h * STEPS : (h + 1) * STEPS]

    share = attended.shape[2]

    def scatter(terms, sums, n, k):
        out = jnp.dot(mixed[...].astype(BF16), wv[...], preferred_element_type=F32)
        for to in range(TP):
            terms[to] = out[:n, to * share : (to + 1) * share]
        copies = []
        for i in range(1, TP):
            to = lax.rem(tp + i, TP)
            copy = pltpu.make_async_remote_copy(
                terms.at[to], sums.at[i], p_send.at[k, i], p_recv.at[k, i],
                device_id={"tp": to}, device_id_type=MESH,
            )
            copy.start()
            copies.append(copy)
        sums[0] = terms[tp]
        return copies

    mixed[...] = jnp.zeros_like(mixed)
    for r in range(RES):
        write_tokens(r, 0, res_k.at[r])
        weigh(r, res_k.at[r])
        mix(r, res_v.at[r], r * STEPS)
        write_tokens(r, 1, res_v.at[r])

    wait_bytes(r_sem.at[0, 0], spread_k.at[pl.ds(1, INST - 1)])
    send_second(0)
    loads[8].wait()
    copies = scatter(part, got, RES * STEPS, 0)
    wait_bytes(r_sem.at[0, 1], spread_v.at[pl.ds(1, INST - 1)])
    send_second(1)
    for copy in copies:
        copy.wait()
    total = jnp.sum(got[...], axis=0)
    for r in range(RES):
        attended[r] = total[r * STEPS : (r + 1) * STEPS].astype(attended.dtype)

    wait_bytes(r_sem.at[1, 0], arr.at[0, sent])
    write_tokens(RES, 0, arr.at[0])
    weigh(RES, arr.at[0])
    for c in range(2):
        wait_bytes(s_sem.at[0, c], arr.at[c, sent])
    wait_bytes(s_sem.at[1, 0], arr.at[0, sent])
    for c in range(2):
        for r in range(RES + 1 - c):
            pltpu.make_async_copy(res_k.at[0], (ko, vo)[c].at[r], o_sem.at[c, r]).wait()

    wait_bytes(r_sem.at[1, 1], arr.at[1, sent])
    mix(RES, arr.at[1], 0)
    copies = scatter(part_l, got_l, STEPS, 1)
    write_tokens(RES, 1, arr.at[1])
    wait_bytes(s_sem.at[1, 1], arr.at[1, sent])
    pltpu.make_async_copy(arr.at[1], vo.at[RES], o_sem.at[1, RES]).wait()
    for copy in copies:
        copy.wait()
    attended[RES] = jnp.sum(got_l[...], axis=0).astype(attended.dtype)


def put(*refs):
    n = len(refs) // 2
    copies = [pltpu.make_async_copy(refs[i], refs[n + i], refs[-1].at[i]) for i in range(n)]
    for copy in copies:
        copy.start()
    for copy in copies:
        copy.wait()


def local(queries, keys_new, values_new, key_cache, value_cache, lengths, migration, out_weight):
    rows = queries.shape[0]
    share = out_weight.shape[1] // TP
    hbm, vmem, anywhere = (pl.BlockSpec(memory_space=m) for m in (pltpu.HBM, pltpu.VMEM, pl.ANY))
    cache = (WINDOW, HEAD)
    n_q = rows * HEADS * STEPS
    migration = migration.T
    shapes = [((rows, STEPS, share), BF16), ((rows, *cache), BF16), ((rows, *cache), BF16)]
    outs = pl.pallas_call(
        kernel,
        out_shape=[pltpu.VMEM(*s) for s in shapes],
        in_specs=[hbm] * 8,
        out_specs=[vmem, anywhere, anywhere],
        scratch_shapes=[
            pltpu.SMEM(lengths.shape, jnp.int32),
            pltpu.SMEM(migration.shape, jnp.int32),
            pltpu.VMEM(migration.shape, jnp.int32),
            pltpu.VMEM(queries.shape, BF16),
            pltpu.VMEM(keys_new.shape, BF16),
            pltpu.VMEM(values_new.shape, BF16),
            pltpu.VMEM((RES, *cache), BF16),
            pltpu.VMEM((RES, *cache), BF16),
            pltpu.VMEM((2, *cache), BF16),
            pltpu.VMEM((2, *cache), BF16),
            pltpu.VMEM((INST, PIECE, HEAD), BF16),
            pltpu.VMEM((INST, PIECE, HEAD), BF16),
            pltpu.VMEM((2, *cache), BF16),
            pltpu.VMEM(out_weight.shape, BF16),
            pltpu.VMEM((INST, 128), jnp.int32),
            pltpu.SMEM((INST, 128), jnp.int32),
            pltpu.VMEM((n_q, HEAD), F32),
            pltpu.VMEM((rows * STEPS, HEAD), F32),
            pltpu.VMEM((rows, HEADS * STEPS, WINDOW), F32),
            pltpu.VMEM((STEPS, HEADS * STEPS, HEAD), F32),
            pltpu.VMEM((8, HEADS * HEAD), F32),
            pltpu.VMEM((TP, RES * STEPS, share), F32),
            pltpu.VMEM((TP, RES * STEPS, share), F32),
            pltpu.VMEM((TP, STEPS, share), F32),
            pltpu.VMEM((TP, STEPS, share), F32),
            pltpu.SemaphoreType.DMA((9,)),
            pltpu.SemaphoreType.DMA,
            pltpu.SemaphoreType.DMA((2, 2)),
            pltpu.SemaphoreType.DMA((2, 2)),
            pltpu.SemaphoreType.DMA((2, rows)),
            pltpu.SemaphoreType.DMA((2, TP)),
            pltpu.SemaphoreType.DMA((2, TP)),
        ],
        compiler_params=pltpu.CompilerParams(
            collective_id=0, has_side_effects=True, vmem_limit_bytes=24 << 20
        ),
        cost_estimate=pl.CostEstimate(flops=50_000_000, bytes_accessed=8 << 20, transcendentals=40_000),
    )(*(
        pltpu.with_memory_space_constraint(v, pltpu.HBM)
        for v in (lengths, migration, queries, keys_new, values_new, key_cache, value_cache, out_weight)
    ))
    return pl.pallas_call(
        put,
        out_shape=[jax.ShapeDtypeStruct(*s) for s in shapes],
        in_specs=[anywhere] * 3,
        out_specs=[anywhere] * 3,
        scratch_shapes=[pltpu.SemaphoreType.DMA((3,))],
        compiler_params=pltpu.CompilerParams(vmem_limit_bytes=1 << 20),
        cost_estimate=pl.CostEstimate(flops=0, bytes_accessed=4 << 20, transcendentals=0),
    )(*(pltpu.with_memory_space_constraint(v, pltpu.VMEM) for v in outs))


def solution(mesh):
    in_specs = (
        P("inst", None, "tp"),
        P("inst", None, "tp"),
        P("inst", None, "tp"),
        P("inst", None, "tp"),
        P("inst", None, "tp"),
        P(),
        P(),
        P("tp", None),
    )
    out_specs = (P("inst", None, "tp"), P("inst", None, "tp"), P("inst", None, "tp"))
    return jax.shard_map(local, mesh=mesh, in_specs=in_specs, out_specs=out_specs, check_vma=False)
```

time: 252 us -> 73.2 us (0.29); the launches traced: 248 us -> 73.1 us
  other arithmetic: 74.7 us -> 0 us
  Pallas kernels: 0 us -> 72.5 us
  starting transfers between devices: 50 us -> 0 us
  local copies, waits for them, and re-layouts: 43.6 us -> 0 us
  waiting for transfers between devices: 40.4 us -> 0 us
  blocking collectives: 26 us -> 0 us
  matrix products: 6.97 us -> 0 us
  between operations: 5.96 us -> 0.64 us
    pallas_call x0 -> x2, Pallas kernels: none -> 72.5 us  [the longest x1 71.1 us: local(): pl.pallas_call(kernel, out_shape=[pltpu.VMEM(*s) for s in shapes], in_spe...]
    all_to_all x4 -> x0, starting transfers between devices: 50 us -> none  [the longest x1 19.1 us: local(): lax.all_to_all(moving_keys, 'inst', split_axis=0, concat_axis=0, tiled=True)]
    scatter x17 -> x0, other arithmetic: 47.9 us -> none
    all_to_all x4 -> x0, waiting for transfers between devices: 40.4 us -> none  [the longest x1 14.9 us: local(): lax.all_to_all(ordered_values, 'inst', split_axis=0, concat_axis=0, tiled...]
    scatter x24 -> x0, local copies, waits for them, and re-layouts: 32 us -> none
    psum x1 -> x0, blocking collectives: 26 us -> none  [local(): summed = lax.psum(partial_value, 'tp')]
    concatenate x8 -> x0, other arithmetic: 8.04 us -> none  [the longest x1 2.28 us: local(): value_rows = jnp.concatenate([value_cache, arrived_values], axis=0)]
    dot_general x9 -> x0, matrix products: 6.97 us -> none  [the longest x2 2.58 us: attend(): jnp.einsum('stgrl,slgd->stgrd', cache_probs, cache_values, preferred_elem...]
  transfers between devices with their start and end apart: 4 -> 0, of which waited for: 3 -> 0; matrix products, arithmetic and copies ran while one was open for 12% -> 0% of each run, Pallas kernels for 0% -> 0%
where the time goes in v1:
time: 73.2 us; the launch traced here: 73.1 us
  Pallas kernels  72.5 us (99%)
    pallas_call x1, Pallas kernels, local(): pl.pallas_call(kernel, out_shape=[pltpu.VMEM(*s) for s in shapes], in_spe...  71.1 us

profile of v1, /device:TPU:1, one launch (start us, length us, event | category | flops | bytes accessed | tf_op | source)
XLA Modules:
  0.0 73.1 jit_solution(7472745801880607861)
XLA Ops:
  0.6 71.1 %shard_map.103 = (bf16[4,2,384]{2,1,0:T(2,128)(2,1)S(1)}, bf16[4,1024,128]{2,1,0:T(8,128)(2,1)S(1)}, bf16[4,1024,128]{2,1,0:T(8,128)(2,1)S(1)}) custom-call(s32[192]{0:T(256)} %lengths_h.1, s32[2,64]{1,0:T(2,128)} %bitcast.1, bf16[4,2,512]{2,1,0:T(2,128)(2,1)} %queries_h.1, bf16[4,2,128]{2,1,0:T(2,128)(2,1)} %keys_h.1, bf16[4,2,128]{2,1,0:T(2,128)(2,1)} %values_h.1, ...), custom_call_target="tpu_custom_call" | custom-call | flops 50000000 | bytes 8388608 | tf_op jit(solution)/shard_map/pallas_call | solution.py:266
  71.8 1.3 %shard_map.104 = (bf16[4,2,384]{2,1,0:T(2,128)(2,1)}, bf16[4,1024,128]{2,1,0:T(8,128)(2,1)}, bf16[4,1024,128]{2,1,0:T(8,128)(2,1)}) custom-call(bf16[4,2,384]{2,1,0:T(2,128)(2,1)S(1)} %get-tuple-element.6.refs_0_, bf16[4,1024,128]{2,1,0:T(8,128)(2,1)S(1)} %get-tuple-element.7.refs_1_, bf16[4,1024,128]{2,1,0:T(8,128)(2,1)S(1)} %get-tuple-element.8.refs_2_), custom_call_target="tpu_custom_call" | custom-call | bytes 4194304 | tf_op jit(solution)/shard_map/pallas_call | solution.py:313

commit v2 on v1

--- a/solution.py
+++ b/solution.py
@@ -17,6 +17,7 @@
 WINDOW = 1024
 PIECE = WINDOW // INST
 STEPS = 2
+FIRST = (0, 2, 4, 16)
 HEADS = 4
 F32 = jnp.float32
 BF16 = jnp.bfloat16
@@ -94,15 +95,21 @@
 
         lax.fori_loop(0, INST, pick, 0)
 
-        def step(j, _):
+        def step(low, high, j, _):
             _, d = peer(j, x, z)
-            pltpu.make_async_remote_copy(
-                ordered.at[c, rows_of(d)], arr.at[c, rows_of(me)], s_sem.at[1, c], r_sem.at[1, c],
-                device_id={"inst": d}, device_id_type=MESH,
-            ).start()
+            zd = lax.rem(d, ZS)
+
+            @pl.when(jnp.logical_and(zd >= low, zd < high))
+            def _():
+                pltpu.make_async_remote_copy(
+                    ordered.at[c, rows_of(d)], arr.at[c, rows_of(me)], s_sem.at[1, c], r_sem.at[1, c],
+                    device_id={"inst": d}, device_id_type=MESH,
+                ).start()
+
             return 0
 
-        lax.fori_loop(0, INST - 1, step, 0)
+        for low, high in zip(FIRST, FIRST[1:]):
+            lax.fori_loop(0, INST - 1, functools.partial(step, low, high), 0)
         arr[c, rows_of(me)] = ordered[c, rows_of(me)]
 
     def wait_bytes(sem, buf):
@@ -194,17 +201,12 @@
         out = jnp.dot(mixed[...].astype(BF16), wv[...], preferred_element_type=F32)
         for to in range(TP):
             terms[to] = out[:n, to * share : (to + 1) * share]
-        copies = []
-        for i in range(1, TP):
+        for i in (4, 3, 5, 2, 6, 1, 7):
             to = lax.rem(tp + i, TP)
-            copy = pltpu.make_async_remote_copy(
-                terms.at[to], sums.at[i], p_send.at[k, i], p_recv.at[k, i],
-                device_id={"tp": to}, device_id_type=MESH,
-            )
-            copy.start()
-            copies.append(copy)
+            pltpu.make_async_remote_copy(
+                terms.at[to], sums.at[i], p_send.at[k], p_recv.at[k], device_id={"tp": to}, device_id_type=MESH
+            ).start()
         sums[0] = terms[tp]
-        return copies
 
     mixed[...] = jnp.zeros_like(mixed)
     for r in range(RES):
@@ -216,11 +218,11 @@
     wait_bytes(r_sem.at[0, 0], spread_k.at[pl.ds(1, INST - 1)])
     send_second(0)
     loads[8].wait()
-    copies = scatter(part, got, RES * STEPS, 0)
+    scatter(part, got, RES * STEPS, 0)
     wait_bytes(r_sem.at[0, 1], spread_v.at[pl.ds(1, INST - 1)])
     send_second(1)
-    for copy in copies:
-        copy.wait()
+    others = pl.ds(1, TP - 1)
+    wait_bytes(p_recv.at[0], got.at[others])
     total = jnp.sum(got[...], axis=0)
     for r in range(RES):
         attended[r] = total[r * STEPS : (r + 1) * STEPS].astype(attended.dtype)
@@ -237,13 +239,14 @@
 
     wait_bytes(r_sem.at[1, 1], arr.at[1, sent])
     mix(RES, arr.at[1], 0)
-    copies = scatter(part_l, got_l, STEPS, 1)
+    scatter(part_l, got_l, STEPS, 1)
     write_tokens(RES, 1, arr.at[1])
+    wait_bytes(p_send.at[0], part.at[others])
+    wait_bytes(p_recv.at[1], got_l.at[others])
+    attended[RES] = jnp.sum(got_l[...], axis=0).astype(attended.dtype)
+    pltpu.make_async_copy(arr.at[1], vo.at[RES], o_sem.at[1, RES]).wait()
     wait_bytes(s_sem.at[1, 1], arr.at[1, sent])
-    pltpu.make_async_copy(arr.at[1], vo.at[RES], o_sem.at[1, RES]).wait()
-    for copy in copies:
-        copy.wait()
-    attended[RES] = jnp.sum(got_l[...], axis=0).astype(attended.dtype)
+    wait_bytes(p_send.at[1], part_l.at[others])
 
 
 def put(*refs):
@@ -299,8 +302,8 @@
             pltpu.SemaphoreType.DMA((2, 2)),
             pltpu.SemaphoreType.DMA((2, 2)),
             pltpu.SemaphoreType.DMA((2, rows)),
-            pltpu.SemaphoreType.DMA((2, TP)),
-            pltpu.SemaphoreType.DMA((2, TP)),
+            pltpu.SemaphoreType.DMA((2,)),
+            pltpu.SemaphoreType.DMA((2,)),
         ],
         compiler_params=pltpu.CompilerParams(
             collective_id=0, has_side_effects=True, vmem_limit_bytes=24 << 20

time: 73.2 us -> 70.1 us (0.958)
  Pallas kernels: 72.5 us -> 68.7 us
    pallas_call x1, Pallas kernels: 71.1 us -> 67.4 us  [local(): pl.pallas_call(kernel, out_shape=[pltpu.VMEM(*s) for s in shapes], in_spe...]
where the time goes in v2:
time: 70.1 us; the launch traced here: 69.4 us
  Pallas kernels  68.7 us (98%)
    pallas_call x1, Pallas kernels, local(): pl.pallas_call(kernel, out_shape=[pltpu.VMEM(*s) for s in shapes], in_spe...  67.4 us

profile of v2, /device:TPU:1, one launch (start us, length us, event | category | flops | bytes accessed | tf_op | source)
XLA Modules:
  0.0 69.4 jit_solution(17398704285522557705)
XLA Ops:
  0.6 67.4 %shard_map.103 = (bf16[4,2,384]{2,1,0:T(2,128)(2,1)S(1)}, bf16[4,1024,128]{2,1,0:T(8,128)(2,1)S(1)}, bf16[4,1024,128]{2,1,0:T(8,128)(2,1)S(1)}) custom-call(s32[192]{0:T(256)} %lengths_h.1, s32[2,64]{1,0:T(2,128)} %bitcast.1, bf16[4,2,512]{2,1,0:T(2,128)(2,1)} %queries_h.1, bf16[4,2,128]{2,1,0:T(2,128)(2,1)} %keys_h.1, bf16[4,2,128]{2,1,0:T(2,128)(2,1)} %values_h.1, ...), custom_call_target="tpu_custom_call" | custom-call | flops 50000000 | bytes 8388608 | tf_op jit(solution)/shard_map/pallas_call | solution.py:269
  68.0 1.3 %shard_map.104 = (bf16[4,2,384]{2,1,0:T(2,128)(2,1)}, bf16[4,1024,128]{2,1,0:T(8,128)(2,1)}, bf16[4,1024,128]{2,1,0:T(8,128)(2,1)}) custom-call(bf16[4,2,384]{2,1,0:T(2,128)(2,1)S(1)} %get-tuple-element.6.refs_0_, bf16[4,1024,128]{2,1,0:T(8,128)(2,1)S(1)} %get-tuple-element.7.refs_1_, bf16[4,1024,128]{2,1,0:T(8,128)(2,1)S(1)} %get-tuple-element.8.refs_2_), custom_call_target="tpu_custom_call" | custom-call | bytes 4194304 | tf_op jit(solution)/shard_map/pallas_call | solution.py:316

commit v3 on v2

--- a/solution.py
+++ b/solution.py
@@ -198,11 +198,13 @@
     share = attended.shape[2]
 
     def scatter(terms, sums, n, k):
-        out = jnp.dot(mixed[...].astype(BF16), wv[...], preferred_element_type=F32)
-        for to in range(TP):
-            terms[to] = out[:n, to * share : (to + 1) * share]
-        for i in (4, 3, 5, 2, 6, 1, 7):
+        rows = mixed[...].astype(BF16)
+        for i in (4, 3, 5, 2, 6, 1, 7, 0):
             to = lax.rem(tp + i, TP)
+            cols = pl.ds(pl.multiple_of(to * share, 128), share)
+            terms[to] = jnp.dot(rows, wv[:, cols], preferred_element_type=F32)[:n]
+            if i == 0:
+                continue
             pltpu.make_async_remote_copy(
                 terms.at[to], sums.at[i], p_send.at[k], p_recv.at[k], device_id={"tp": to}, device_id_type=MESH
             ).start()

time: 70.1 us -> 69.9 us (level)
  no operation moved by 1% of the time
where the time goes in v3:
time: 69.9 us; the launch traced here: 69.1 us
  Pallas kernels  68.5 us (98%)
    pallas_call x1, Pallas kernels, local(): pl.pallas_call(kernel, out_shape=[pltpu.VMEM(*s) for s in shapes], in_spe...  67.1 us

profile of v3, /device:TPU:1, one launch (start us, length us, event | category | flops | bytes accessed | tf_op | source)
XLA Modules:
  0.0 69.1 jit_solution(16036539032545538426)
XLA Ops:
  0.6 67.1 %shard_map.103 = (bf16[4,2,384]{2,1,0:T(2,128)(2,1)S(1)}, bf16[4,1024,128]{2,1,0:T(8,128)(2,1)S(1)}, bf16[4,1024,128]{2,1,0:T(8,128)(2,1)S(1)}) custom-call(s32[192]{0:T(256)} %lengths_h.1, s32[2,64]{1,0:T(2,128)} %bitcast.1, bf16[4,2,512]{2,1,0:T(2,128)(2,1)} %queries_h.1, bf16[4,2,128]{2,1,0:T(2,128)(2,1)} %keys_h.1, bf16[4,2,128]{2,1,0:T(2,128)(2,1)} %values_h.1, ...), custom_call_target="tpu_custom_call" | custom-call | flops 50000000 | bytes 8388608 | tf_op jit(solution)/shard_map/pallas_call | solution.py:271
  67.8 1.3 %shard_map.104 = (bf16[4,2,384]{2,1,0:T(2,128)(2,1)}, bf16[4,1024,128]{2,1,0:T(8,128)(2,1)}, bf16[4,1024,128]{2,1,0:T(8,128)(2,1)}) custom-call(bf16[4,2,384]{2,1,0:T(2,128)(2,1)S(1)} %get-tuple-element.6.refs_0_, bf16[4,1024,128]{2,1,0:T(8,128)(2,1)S(1)} %get-tuple-element.7.refs_1_, bf16[4,1024,128]{2,1,0:T(8,128)(2,1)S(1)} %get-tuple-element.8.refs_2_), custom_call_target="tpu_custom_call" | custom-call | bytes 4194304 | tf_op jit(solution)/shard_map/pallas_call | solution.py:318
